TPU v7x, 32 devices: a whole 2x2x4 slice. The times are simulated.
32 devices in a mesh: dp: 8 (over y, x, core), ctx: 4 (over z).
Axes of the slice: x: 2, y: 2, z: 4, core: 2. Of those that a mesh axis runs over, the one named last changes fastest.
Arguments:
- queries: bfloat16 [8, 4096, 512], P('dp', 'ctx'), may hold values from -6 to 6
- keys: bfloat16 [8, 4096, 128], P('dp', 'ctx'), may hold values from -6 to 6
- values: bfloat16 [8, 4096, 128], P('dp', 'ctx'), may hold values from -6 to 6
- dest_replica: int32 [8, 64], P('dp', 'ctx'), may hold values from 0 to 7, as said below
- dest_slot: int32 [8, 64], P('dp', 'ctx'), may hold values from 0 to 63, as said below
- doc_lengths: int32 [8, 16], P('dp'), may hold values from 1 to 32, 64 in all within a row
- tile_mask: int32 [8, 64, 64], P('dp', 'ctx'), may hold values 0 or 1
Outputs:
- attended: bfloat16 [8, 4096, 512], P('dp', 'ctx')
Inputs may be any that keep to these rules, and one draw needn't show every extreme that they name: `dest_replica`: every block of a pack receives exactly one arriving block; a block keeps its shard along ctx (dest_slot // 16 equals the arriving block's own b // 16); the 16 blocks of one device go to every pack, 2 to each. `dest_slot`: see dest_replica. `doc_lengths`: they sum to 64 in every pack, and the largest is 32 in every pack.
All inputs are finite; a program needn't handle non-finite values. No bound on the sum of `tile_mask` on one device may be relied on, other than what follows from the above.
Results may differ from a plain program's by a relative error of at most 0.0033.
Values may be sent and summed in bfloat16 or wider, within the bound.
No kernel may reach another device: no remote copies, remote signals or barrier semaphores. Data moves between devices by JAX's collectives and lax.ppermute only.
A program may use at most 64 MiB of HBM per device.

v0:
```python
import jax
import jax.numpy as jnp
from jax import lax
from jax.sharding import PartitionSpec as P

HEAD_WIDTH = 128
QUERY_HEADS = 4
KEY_VALUE_HEADS = 1
REACH = 2


def shifted(value, axis, steps):
    count = lax.axis_size(axis)
    leading, last = (max(0, -steps), min(count, count - steps))
    return lax.ppermute(value, axis, [(source, source + steps) for source in range(leading, last)])


def block_docs(ends, block_ids):
    return jnp.sum((ends[None, :] <= block_ids[:, None]).astype(jnp.int32), axis=1)


def shard_attend(rows_of_queries, rows_of_keys, rows_of_values, allowed):
    count_of_rows = rows_of_queries.shape[0]
    query_group_width = QUERY_HEADS // KEY_VALUE_HEADS
    heads_of_queries = rows_of_queries.reshape(
        count_of_rows, KEY_VALUE_HEADS, query_group_width, HEAD_WIDTH
    )
    heads_of_keys = rows_of_keys.reshape(rows_of_keys.shape[0], KEY_VALUE_HEADS, HEAD_WIDTH)
    heads_of_values = rows_of_values.reshape(rows_of_values.shape[0], KEY_VALUE_HEADS, HEAD_WIDTH)
    scores = jnp.einsum(
        "qhgd,khd->hgqk", heads_of_queries, heads_of_keys, preferred_element_type=jnp.float32
    ) * HEAD_WIDTH ** (-0.5)
    masked = jnp.where(allowed, scores, -jnp.inf)
    row_max = jnp.max(masked, axis=-1)
    present = jnp.any(allowed, axis=-1)
    safe_max = jnp.where(present, row_max, 0.0)
    weights = jnp.where(allowed, jnp.exp(scores - safe_max[..., None]), 0.0)
    row_sum = jnp.sum(weights, axis=-1)
    partial_value = jnp.einsum(
        "hgqk,khd->qhgd",
        weights.astype(jnp.bfloat16),
        heads_of_values,
        preferred_element_type=jnp.float32,
    )
    return (row_max, row_sum, partial_value)


def combine(portions):
    overall = portions[0][0]
    for portion in portions[1:]:
        overall = jnp.maximum(overall, portion[0])
    denominator = jnp.zeros_like(overall)
    numerator = jnp.zeros_like(portions[0][2])
    for portion in portions:
        factor = jnp.exp(portion[0] - overall)
        denominator = denominator + factor * portion[1]
        numerator = numerator + jnp.transpose(factor, (2, 0, 1))[..., None] * portion[2]
    result = numerator / jnp.transpose(denominator, (2, 0, 1))[..., None]
    return result.reshape(result.shape[0], -1).astype(jnp.bfloat16)


def per_device(queries, keys, values, dest_replica, dest_slot, doc_lengths, tile_mask):
    token_count = queries.shape[1]
    block_count = dest_replica.shape[1]
    block_len = token_count // block_count
    replica_count = lax.axis_size("dp")
    per_pack = block_count // replica_count
    column = lax.axis_index("ctx")
    targets = dest_replica[0]
    local_slot = dest_slot[0] - column * block_count
    block_index = jnp.arange(block_count, dtype=jnp.int32)
    same_target = targets[:, None] == targets[None, :]
    earlier = block_index[None, :] < block_index[:, None]
    ranking = jnp.sum((same_target & earlier).astype(jnp.int32), axis=1)
    select = targets[None, None, :] == jnp.arange(replica_count, dtype=jnp.int32)[:, None, None]
    select = select & (
        ranking[None, None, :] == jnp.arange(per_pack, dtype=jnp.int32)[None, :, None]
    )
    select_matrix = select.astype(jnp.bfloat16)
    slot_send = jnp.sum(select.astype(jnp.int32) * (local_slot + 1)[None, None, :], axis=2) - 1

    def pack_blocks(array):
        blocks = array[0].reshape(block_count, block_len, array.shape[2])
        return jnp.einsum(
            "kcj,jbf->kcbf", select_matrix, blocks, preferred_element_type=jnp.float32
        ).astype(jnp.bfloat16)

    def place_blocks(received, slots_in):
        placer = (slots_in[None, :, :] == block_index[:, None, None]).astype(jnp.bfloat16)
        placed = jnp.einsum(
            "jsc,scbf->jbf", placer, received, preferred_element_type=jnp.float32
        ).astype(jnp.bfloat16)
        return placed.reshape(token_count, received.shape[3])

    incoming_q, incoming_k, incoming_v, incoming_slots = (
        lax.all_to_all(pack_blocks(queries), "dp", split_axis=0, concat_axis=0, tiled=True),
        lax.all_to_all(pack_blocks(keys), "dp", split_axis=0, concat_axis=0, tiled=True),
        lax.all_to_all(pack_blocks(values), "dp", split_axis=0, concat_axis=0, tiled=True),
        lax.all_to_all(slot_send, "dp", split_axis=0, concat_axis=0, tiled=True),
    )
    routed_k = place_blocks(incoming_k, incoming_slots)
    routed_v = place_blocks(incoming_v, incoming_slots)
    routed_q = place_blocks(incoming_q, incoming_slots)
    ends = jnp.cumsum(doc_lengths[0])
    query_blocks = column * block_count + block_index
    query_docs = block_docs(ends, query_blocks)
    token_index = jnp.arange(token_count, dtype=jnp.int32)
    query_pos = column * token_count + token_index
    mask_rows = tile_mask[0]

    def allowed_for(offset):
        key_blocks = (column - offset) * block_count + block_index
        key_docs = block_docs(ends, key_blocks)
        start = jnp.maximum(column - offset, 0) * block_count
        mask_cols = lax.dynamic_slice_in_dim(mask_rows, start, block_count, 1)
        tile_ok = (query_docs[:, None] == key_docs[None, :]) & (
            key_blocks[None, :] <= query_blocks[:, None]
        )
        tile_ok = tile_ok & ((mask_cols == 1) | (key_blocks[None, :] == query_blocks[:, None]))
        tile_ok = tile_ok & (key_blocks[None, :] >= 0)
        expanded = jnp.repeat(jnp.repeat(tile_ok, block_len, axis=0), block_len, axis=1)
        key_pos = (column - offset) * token_count + token_index
        return expanded & (key_pos[None, :] <= query_pos[:, None])

    portions = [shard_attend(routed_q, routed_k, routed_v, allowed_for(0))]
    stacked_kv = jnp.stack((routed_k, routed_v))
    moving = stacked_kv
    for offset in range(1, REACH + 1):
        moving = shifted(moving, "ctx", 1)
        allowed = allowed_for(offset)
        portions.append(shard_attend(routed_q, moving[0], moving[1], allowed))
    return combine(portions)[None]


def solution(mesh):
    return jax.shard_map(
        per_device,
        mesh=mesh,
        in_specs=(
            P("dp", "ctx", None),
            P("dp", "ctx", None),
            P("dp", "ctx", None),
            P("dp", "ctx"),
            P("dp", "ctx"),
            P("dp", None),
            P("dp", "ctx", None),
        ),
        out_specs=P("dp", "ctx", None),
        check_vma=False,
    )
```

profile of v0, /device:TPU:0, one launch (start us, length us, event | category | flops | bytes accessed | tf_op | source)
XLA Modules:
  0.0 122.6 jit_solution(3238020268207875446)
XLA Ops:
  0.0 0.9 convert_reduce_fusion.2
  0.9 0.7 iota_compare_fusion.2
  1.6 0.7 add_bitcast_fusion.1
  2.3 0.1 fusion.53
  2.4 0.7 copy.69
  3.1 5.2 %all-to-all-start = ((s32[8,1,2]{2,1,0:T(1,128)}), s32[8,1,2]{2,1,0:T(1,128)S(1)}, u32[]{:S(2)}, u32[]{:S(2)}) async-start(s32[8,1,2]{2,1,0:T(1,128)} %copy.69), calls=%async_computation | async-start | bytes 8192 | tf_op jit(solution)/shard_map/all_to_all | solution.py:99
  8.3 0.7 copy.67
  9.1 0.1 reduce.9
  9.2 1.2 convolution_convert_fusion.2
  10.4 0.9 copy.72
  11.4 1.2 convolution_convert_fusion.1
  12.6 0.7 convolution_convert_fusion
  13.3 0.2 convert_reduce_fusion
  13.5 4.2 %all-to-all-start.1 = ((bf16[8,2,64,128]{3,1,2,0:T(2,128)(2,1)}), bf16[8,2,64,128]{3,1,2,0:T(2,128)(2,1)S(1)}, u32[]{:S(2)}, u32[]{:S(2)}) async-start(bf16[8,2,64,128]{3,1,2,0:T(2,128)(2,1)} %copy.72), calls=%async_computation.1 | async-start | bytes 524288 | tf_op jit(solution)/shard_map/all_to_all | solution.py:97
  17.7 0.9 fusion.60
  18.9 0.1 broadcast_in_dim.56
  19.0 0.1 reshape.479
  19.1 0.1 broadcast_in_dim.59
  19.2 0.1 reshape.482
  19.3 0.1 broadcast_in_dim.52
  19.4 0.1 reshape.475
  19.6 0.9 copy.83
  20.5 1.8 %copy.76 = bf16[8,2,64,512]{3,1,2,0:T(2,128)(2,1)} copy(bf16[8,2,64,512]{3,0,1,2:T(8,128)(2,1)S(1)} %convolution_convert_fusion) | data formatting | bytes 2097152 | tf_op jit(solution)/shard_map/convert_element_type | solution.py:86
  22.2 2.5 %bitcast_and_fusion = (pred[1024,1024]{0,1:T(8,128)(4,1)S(1)}, pred[1024,1024]{0,1:T(8,128)(4,1)S(1)}, pred[1024,1024]{0,1:T(8,128)(4,1)S(1)}) fusion(s32[1024]{0:T(1024)S(1)} %iota_add_fusion.2, s32[1024]{0:T(1024)S(1)} %get-tuple-element.31, pred[1024,16]{0,1:T(8,128)(4,1)S(1)} %reshape.482, pred[1024,16]{0,1:T(8,128)(4,1)S(1)} %reshape.475, ...), kind=kLoop, calls=%fused_computation.30 | loop fusion | flops 6291456 | bytes 3207168 | tf_op jit(solution)/shard_map/and | solution.py:123
  24.8 4.2 %all-to-all-start.3 = ((bf16[8,2,64,128]{3,1,2,0:T(2,128)(2,1)}), bf16[8,2,64,128]{3,1,2,0:T(2,128)(2,1)}, u32[]{:S(2)}, u32[]{:S(2)}) async-start(bf16[8,2,64,128]{3,1,2,0:T(2,128)(2,1)} %copy.83), calls=%async_computation.3 | async-start | bytes 524288 | tf_op jit(solution)/shard_map/all_to_all | solution.py:98
  29.0 0.4 fusion.33
  29.4 0.8 copy.74
  30.2 5.9 %all-to-all-done.3 = bf16[8,2,64,128]{3,1,2,0:T(2,128)(2,1)} async-done(((bf16[8,2,64,128]{3,1,2,0:T(2,128)(2,1)}), bf16[8,2,64,128]{3,1,2,0:T(2,128)(2,1)}, u32[]{:S(2)}, u32[]{:S(2)}) %all-to-all-start.3) | async-done | bytes 262176 | tf_op jit(solution)/shard_map/all_to_all | solution.py:98
  36.1 4.2 %all-to-all-start.2 = ((bf16[8,2,64,512]{3,1,2,0:T(2,128)(2,1)}), bf16[8,2,64,512]{3,1,2,0:T(2,128)(2,1)}, u32[]{:S(2)}, u32[]{:S(2)}) async-start(bf16[8,2,64,512]{3,1,2,0:T(2,128)(2,1)} %copy.76), calls=%async_computation.2 | async-start | bytes 2097152 | tf_op jit(solution)/shard_map/all_to_all | solution.py:96
  40.3 1.3 %fusion.34 = bf16[16,64,128]{2,0,1:T(8,128)(2,1)S(1)} fusion(bf16[8,2,64,128]{3,1,2,0:T(2,128)(2,1)} %all-to-all-done.3, s32[8,2]{0,1:T(2,128)S(1)} %bitcast.293), kind=kOutput, calls=%fused_computation.48 | convolution fusion | flops 4325632 | bytes 524352 | tf_op jit(solution)/shard_map/jsc,scbf->jbf/dot_general | solution.py:90
  41.7 1.0 pad_maximum_fusion
  42.7 4.3 %collective-permute-start = (bf16[2,1024,128]{2,1,0:T(8,128)(2,1)S(1)}, bf16[2,1024,128]{2,1,0:T(8,128)(2,1)}, u32[]{:S(2)}, u32[]{:S(2)}) collective-permute-start(bf16[2,1024,128]{2,1,0:T(8,128)(2,1)S(1)} %pad_maximum_fusion), channel_id=1, source_target_pairs={{0,1},{1,2},{2,3},{4,5},{5,6},{6,7},{8,9},{9,10},{10,11},{12,13},{... | collective-permute-start | bytes 1572872 | tf_op jit(solution)/shard_map/ppermute | solution.py:15
  47.0 2.4 %and_reduce_fusion = (pred[1024]{0:T(1024)(128)(4,1)S(1)}, pred[1024]{0:T(1024)(128)(4,1)S(1)}, pred[1024]{0:T(1024)(128)(4,1)S(1)}) fusion(s32[16,64]{1,0:T(8,128)S(1)} %get-tuple-element.33, s32[1024]{0:T(1024)S(1)} %iota_add_fusion.2, pred[1024,16]{0,1:T(8,128)(4,1)S(1)} %reshape.482, s32[16,64]{1,0:T(8,128)S(1)} %get-tuple-element.34, ...), kind=kLoop, calls=%fused_computation.33 | loop fusion | flops 9434112 | bytes 68608 | tf_op jit(solution)/shard_map/reduce_or | solution.py:35
  49.4 8.5 %collective-permute-done = bf16[2,1024,128]{2,1,0:T(8,128)(2,1)} collective-permute-done((bf16[2,1024,128]{2,1,0:T(8,128)(2,1)S(1)}, bf16[2,1024,128]{2,1,0:T(8,128)(2,1)}, u32[]{:S(2)}, u32[]{:S(2)}) %collective-permute-start) | collective-permute-done | bytes 524320 | tf_op jit(solution)/shard_map/ppermute | solution.py:15
  57.9 5.3 %collective-permute-start.1 = (bf16[2,1024,128]{2,1,0:T(8,128)(2,1)}, bf16[2,1024,128]{2,1,0:T(8,128)(2,1)}, u32[]{:S(2)}, u32[]{:S(2)}) collective-permute-start(bf16[2,1024,128]{2,1,0:T(8,128)(2,1)} %collective-permute-done), channel_id=1, source_target_pairs={{0,1},{1,2},{2,3},{4,5},{5,6},{6,7},{8,9},{9,10},{10,11},{12,13},{... | collective-permute-start | bytes 1572872 | tf_op jit(solution)/shard_map/ppermute | solution.py:15
  63.2 2.0 %bitcast_convert_fusion = bf16[16,64,512]{2,0,1:T(8,128)(2,1)S(1)} fusion(bf16[8,2,64,512]{3,1,2,0:T(2,128)(2,1)} %all-to-all-done.2, s32[8,2]{0,1:T(2,128)S(1)} %bitcast.294), kind=kOutput, calls=%fused_computation.43 | convolution fusion | flops 17301760 | bytes 2097216 | tf_op jit(solution)/shard_map/jsc,scbf->jbf/dot_general | solution.py:90
  65.2 1.5 %copy.78 = bf16[16,64,512]{2,1,0:T(8,128)(2,1)} copy(bf16[16,64,512]{2,0,1:T(8,128)(2,1)S(1)} %bitcast_convert_fusion) | data formatting | bytes 2097152 | tf_op jit(solution)/shard_map/convert_element_type | solution.py:92
  66.7 2.2 %reshape.478 = bf16[1024,4,128]{2,1,0:T(4,128)(2,1)} reshape(bf16[16,64,512]{2,1,0:T(8,128)(2,1)} %copy.78) | data formatting | bytes 2097152 | tf_op jit(solution)/shard_map/reshape.17
  68.9 4.4 %fusion.6 = (f32[4,1024]{1,0:T(4,128)S(1)}, f32[1024,1024,4]{1,0,2:T(8,128)S(1)}) fusion(pred[1024,1024]{0,1:T(8,128)(4,1)S(1)} %get-tuple-element.19, bf16[1024,128,1]{1,0,2:T(8,128)(2,1)} %bitcast.289, bf16[1024,4,128]{2,1,0:T(4,128)(2,1)} %reshape.478), kind=kOutput, calls=%fused_computation.12 | convolution fusion | flops 1086320640 | bytes 19152896 | tf_op jit(solution)/shard_map/qhgd,khd->hgqk/dot_general | solution.py:30
  73.3 3.7 %fusion.9 = f32[4,1024]{1,0:T(4,128)S(1)} fusion(f32[1024,1024,4]{1,0,2:T(8,128)S(1)} %get-tuple-element.24, f32[4,1024]{1,0:T(4,128)S(1)} %broadcast_select_fusion.2, pred[1024,1024]{0,1:T(8,128)(4,1)S(1)} %get-tuple-element.19), kind=kLoop, calls=%fused_computation.15 | loop fusion | flops 16773120 | bytes 17858560 | tf_op jit(solution)/shard_map/reduce_sum | solution.py:38
  77.0 8.4 %fusion.3 = (f32[4,1024]{1,0:T(4,128)S(1)}, f32[1024,1024,4]{1,0,2:T(8,128)}) fusion(pred[1024,1024]{0,1:T(8,128)(4,1)S(1)} %get-tuple-element.20, bf16[1024,4,128]{2,1,0:T(4,128)(2,1)S(1)} %copy-done.2, bf16[2,1024,128]{2,1,0:T(8,128)(2,1)} %collective-permute-done), kind=kOutput, calls=%fused_computation.7 | convolution fusion | flops 1086320640 | bytes 19152896 | tf_op jit(solution)/shard_map/qhgd,khd->hgqk/dot_general | solution.py:30
  85.4 7.9 %fusion.11 = f32[4,1024]{1,0:T(4,128)S(1)} fusion(f32[1024,1024,4]{1,0,2:T(8,128)} %get-tuple-element.22, f32[4,1024]{1,0:T(4,128)S(1)} %broadcast_select_fusion.1, pred[1024,1024]{0,1:T(8,128)(4,1)S(1)} %get-tuple-element.20), kind=kLoop, calls=%fused_computation.17 | loop fusion | flops 16773120 | bytes 17858560 | tf_op jit(solution)/shard_map/reduce_sum | solution.py:38
  93.4 11.0 %fusion.20 = f32[128,4,1024]{2,0,1:T(8,128)} fusion(f32[1024,1024,4]{1,0,2:T(8,128)} %get-tuple-element.22, f32[4,1024]{1,0:T(4,128)S(1)} %broadcast_select_fusion.1, pred[1024,1024]{0,1:T(8,128)(4,1)S(1)} %get-tuple-element.20, bf16[2,1024,128]{2,1,0:T(8,128)(2,1)} %collective-permute-done), kind=kOutput, calls=%fused_computation.25 | convolution fusion | flops 1090519040 | bytes 20201472 | tf_op jit(solution)/shard_map/hgqk,khd->qhgd/dot_general | solution.py:39
  104.4 3.9 %fusion.18 = f32[128,4,1024]{2,0,1:T(8,128)S(1)} fusion(bf16[1024,128,1]{1,0,2:T(8,128)(2,1)S(1)} %bitcast.287, f32[1024,1024,4]{1,0,2:T(8,128)S(1)} %get-tuple-element.24, f32[4,1024]{1,0:T(4,128)S(1)} %broadcast_select_fusion.2, pred[1024,1024]{0,1:T(8,128)(4,1)S(1)} %get-tuple-element.19), kind=kOutput, calls=%fused_computation.24 | convolution fusion | flops 1090519040 | bytes 20201472 | tf_op jit(solution)/shard_map/hgqk,khd->qhgd/dot_general | solution.py:39
  108.3 4.0 %fusion = (f32[4,1024]{1,0:T(4,128)S(1)}, f32[1024,1024,4]{1,0,2:T(8,128)S(1)}) fusion(pred[1024,1024]{0,1:T(8,128)(4,1)S(1)} %get-tuple-element.18, bf16[1024,4,128]{2,1,0:T(4,128)(2,1)S(1)} %copy-done.2, bf16[2,1024,128]{2,1,0:T(8,128)(2,1)} %collective-permute-done.1), kind=kOutput, calls=%fused_computation.2 | convolution fusion | flops 1086320640 | bytes 19152896 | tf_op jit(solution)/shard_map/qhgd,khd->hgqk/dot_general | solution.py:30
  112.3 3.7 %fusion.13 = f32[4,1024]{1,0:T(4,128)S(1)} fusion(f32[1024,1024,4]{1,0,2:T(8,128)S(1)} %get-tuple-element.26, f32[4,1024]{1,0:T(4,128)S(1)} %broadcast_select_fusion, pred[1024,1024]{0,1:T(8,128)(4,1)S(1)} %get-tuple-element.18), kind=kLoop, calls=%fused_computation.19 | loop fusion | flops 16773120 | bytes 17858560 | tf_op jit(solution)/shard_map/reduce_sum | solution.py:38
  116.1 5.2 %fusion.29 = bf16[1024,1,4,128]{0,3,2,1:T(8,128)(2,1)S(1)} fusion(f32[128,4,1024]{2,0,1:T(8,128)S(1)} %copy-done.3, f32[128,4,1024]{2,0,1:T(8,128)S(1)} %fusion.18, f32[1024,1024,4]{1,0,2:T(8,128)S(1)} %get-tuple-element.26, f32[4,1024]{1,0:T(4,128)S(1)} %broadcast_select_fusion, pred[1024,1024]{0,1:T(8,128)(4,1)S(1)} %get-tuple-element.18, ...), kind=kOutput, calls=%fused_computation.39 | convolution fusion | flops 1094189056 | bytes 23412736 | tf_op jit(solution)/shard_map/hgqk,khd->qhgd/dot_general | solution.py:39
  121.3 1.3 %copy.96 = bf16[1,1024,512]{2,1,0:T(8,128)(2,1)} copy(bf16[1,1024,512]{1,2,0:T(8,128)(2,1)S(1)} %bitcast.285) | data formatting | bytes 2097152 | tf_op jit(solution)/shard_map/convert_element_type | solution.py:59
  (32 shorter events, 0.6 us)
Async XLA Ops:
  0.0 12.6 %copy-start = (bf16[1,1024,512]{2,1,0:T(8,128)(2,1)S(1)}, bf16[1,1024,512]{2,1,0:T(8,128)(2,1)}, u32[]{:S(2)}) copy-start(bf16[1,1024,512]{2,1,0:T(8,128)(2,1)} %param.7) | copy-start | bytes 3145732
  3.1 10.4 %all-to-all-start = ((s32[8,1,2]{2,1,0:T(1,128)}), s32[8,1,2]{2,1,0:T(1,128)S(1)}, u32[]{:S(2)}, u32[]{:S(2)}) async-start(s32[8,1,2]{2,1,0:T(1,128)} %copy.69), calls=%async_computation | async-start | bytes 8192 | tf_op jit(solution)/shard_map/all_to_all | solution.py:99
  13.5 11.3 %all-to-all-start.1 = ((bf16[8,2,64,128]{3,1,2,0:T(2,128)(2,1)}), bf16[8,2,64,128]{3,1,2,0:T(2,128)(2,1)S(1)}, u32[]{:S(2)}, u32[]{:S(2)}) async-start(bf16[8,2,64,128]{3,1,2,0:T(2,128)(2,1)} %copy.72), calls=%async_computation.1 | async-start | bytes 524288 | tf_op jit(solution)/shard_map/all_to_all | solution.py:97
  24.8 11.2 %all-to-all-start.3 = ((bf16[8,2,64,128]{3,1,2,0:T(2,128)(2,1)}), bf16[8,2,64,128]{3,1,2,0:T(2,128)(2,1)}, u32[]{:S(2)}, u32[]{:S(2)}) async-start(bf16[8,2,64,128]{3,1,2,0:T(2,128)(2,1)} %copy.83), calls=%async_computation.3 | async-start | bytes 524288 | tf_op jit(solution)/shard_map/all_to_all | solution.py:98
  36.1 27.1 %all-to-all-start.2 = ((bf16[8,2,64,512]{3,1,2,0:T(2,128)(2,1)}), bf16[8,2,64,512]{3,1,2,0:T(2,128)(2,1)}, u32[]{:S(2)}, u32[]{:S(2)}) async-start(bf16[8,2,64,512]{3,1,2,0:T(2,128)(2,1)} %copy.76), calls=%async_computation.2 | async-start | bytes 2097152 | tf_op jit(solution)/shard_map/all_to_all | solution.py:96
  42.7 15.2 %collective-permute-start = (bf16[2,1024,128]{2,1,0:T(8,128)(2,1)S(1)}, bf16[2,1024,128]{2,1,0:T(8,128)(2,1)}, u32[]{:S(2)}, u32[]{:S(2)}) collective-permute-start(bf16[2,1024,128]{2,1,0:T(8,128)(2,1)S(1)} %pad_maximum_fusion), channel_id=1, source_target_pairs={{0,1},{1,2},{2,3},{4,5},{5,6},{6,7},{8,9},{9,10},{10,11},{12,13},{... | collective-permute-start | bytes 1572872 | tf_op jit(solution)/shard_map/ppermute | solution.py:15
  57.9 50.4 %collective-permute-start.1 = (bf16[2,1024,128]{2,1,0:T(8,128)(2,1)}, bf16[2,1024,128]{2,1,0:T(8,128)(2,1)}, u32[]{:S(2)}, u32[]{:S(2)}) collective-permute-start(bf16[2,1024,128]{2,1,0:T(8,128)(2,1)} %collective-permute-done), channel_id=1, source_target_pairs={{0,1},{1,2},{2,3},{4,5},{5,6},{6,7},{8,9},{9,10},{10,11},{12,13},{... | collective-permute-start | bytes 1572872 | tf_op jit(solution)/shard_map/ppermute | solution.py:15
  68.9 8.1 %copy-start.2 = (bf16[1024,4,128]{2,1,0:T(4,128)(2,1)S(1)}, bf16[1024,4,128]{2,1,0:T(4,128)(2,1)}, u32[]{:S(2)}) copy-start(bf16[1024,4,128]{2,1,0:T(4,128)(2,1)} %reshape.478) | copy-start | bytes 3145732
  112.3 3.7 %copy-start.3 = (f32[128,4,1024]{2,0,1:T(8,128)S(1)}, f32[128,4,1024]{2,0,1:T(8,128)}, u32[]{:S(2)}) copy-start(f32[128,4,1024]{2,0,1:T(8,128)} %fusion.20) | copy-start | bytes 6291460
  116.1 6.6 %copy-start.1 = (bf16[1,1024,512]{2,1,0:T(8,128)(2,1)S(1)}, bf16[1,1024,512]{2,1,0:T(8,128)(2,1)}, u32[]{:S(2)}) copy-start(bf16[1,1024,512]{2,1,0:T(8,128)(2,1)} %param.7) | copy-start | bytes 3145732
where the time goes:
time: 124 us; the launch traced here: 123 us
  matrix products  43.7 us (35%)
  starting transfers between devices  27.4 us (22%)
  other arithmetic  25 us (20%)
  waiting for transfers between devices  14.4 us (12%)
  local copies, waits for them, and re-layouts  11.9 us (10%)
    dot_general x3, matrix products, shard_attend(): jnp.einsum('hgqk,khd->qhgd', weights.astype(jnp.bfloat16), heads_of_value...  20.1 us
    dot_general x3, matrix products, shard_attend(): jnp.einsum('qhgd,khd->hgqk', heads_of_queries, heads_of_keys, preferred_e...  16.8 us
    reduce_sum x3, other arithmetic, shard_attend(): row_sum = jnp.sum(weights, axis=-1)  15.3 us
    ppermute x2, starting transfers between devices, shifted(): lax.ppermute(value, axis, [(source, source + steps) for source in range(l...  9.59 us
    ppermute x2, waiting for transfers between devices, shifted(): lax.ppermute(value, axis, [(source, source + steps) for source in range(l...  8.46 us
    all_to_all x1, waiting for transfers between devices, per_device(): lax.all_to_all(pack_blocks(values), 'dp', split_axis=0, concat_axis=0, ti...  5.89 us
    all_to_all x1, starting transfers between devices, per_device(): lax.all_to_all(slot_send, 'dp', split_axis=0, concat_axis=0, tiled=True)  5.17 us
    all_to_all x1, starting transfers between devices, per_device(): lax.all_to_all(pack_blocks(queries), 'dp', split_axis=0, concat_axis=0, t...  4.23 us
  transfers between devices with their start and end apart: 6, of which 2 were waited for; matrix products, arithmetic and copies ran while one was open for 52% of the time, Pallas kernels for 0%

commit v1 on v0

v1 whole, which is shorter than its diff:
```python
import functools

import jax
import jax.numpy as jnp
from jax import lax
from jax.experimental import pallas as pl
from jax.experimental.pallas import tpu as pltpu
from jax.sharding import PartitionSpec as P

HEAD_WIDTH = 128
QUERY_HEADS = 4
SCALE = HEAD_WIDTH ** (-0.5) * 1.4426950408889634
NEVER = -1e30
FLOOR = -5e29
VMEM_LIMIT = 48 * 1024 * 1024

ANY = pl.BlockSpec(memory_space=pl.ANY)
SMEM = pl.BlockSpec(memory_space=pltpu.SMEM)
VMEM = pl.BlockSpec(memory_space=pltpu.VMEM)


def shifted(value, axis):
    count = lax.axis_size(axis)
    return lax.ppermute(value, axis, [(source, source + 1) for source in range(count - 1)])


def pack_kv_kernel(cap, targets, slots, keys, values, send, table, counts, sem):
    packs = send.shape[0]
    blocks = targets.shape[1]
    size = keys.shape[1] // blocks
    for t in range(packs):
        counts[t] = 0

    def step(j, carry):
        t = targets[0, j]
        rank = counts[t]
        counts[t] = rank + 1
        table[0, t * cap + rank] = lax.rem(slots[0, j], blocks)
        rows = pl.ds(pl.multiple_of(j * size, size), size)
        to = pl.ds(pl.multiple_of(rank * size, size), size)
        pltpu.make_async_copy(keys.at[0, rows], send.at[t, 0, to], sem).start()
        pltpu.make_async_copy(values.at[0, rows], send.at[t, 1, to], sem).start()
        return carry

    lax.fori_loop(0, blocks, step, 0, unroll=True)
    pltpu.make_async_copy(send, send, sem).wait()


def pack_q_kernel(cap, targets, queries, send, counts, sem):
    packs = send.shape[0]
    blocks = targets.shape[1]
    size = queries.shape[1] // blocks
    for t in range(packs):
        counts[t] = 0

    def step(j, carry):
        t = targets[0, j]
        rank = counts[t]
        counts[t] = rank + 1
        rows = pl.ds(pl.multiple_of(j * size, size), size)
        to = pl.ds(pl.multiple_of(rank * size, size), size)
        pltpu.make_async_copy(queries.at[0, rows], send.at[t, to], sem).start()
        return carry

    lax.fori_loop(0, blocks, step, 0, unroll=True)
    pltpu.make_async_copy(send, send, sem).wait()


def first_document(lengths, position):
    start, end = jnp.int32(0), jnp.int32(0)
    total = jnp.int32(0)
    for j in range(lengths.shape[1]):
        after = total + lengths[0, j]
        inside = (total <= position) & (position < after)
        start = jnp.where(inside, total, start)
        end = jnp.where(inside, after, end)
        total = after
    return start, end


def reach_of(lengths, place, offset, blocks):
    start, end = first_document(lengths, place * blocks)
    low = (place - offset) * blocks
    rows = jnp.where(start < low + blocks, jnp.minimum(end - place * blocks, blocks), 0)
    return jnp.where(low >= 0, rows, 0), jnp.maximum(start - low, 0)


def fill_bias(bias, lengths, tiles, place, offset, blocks, size):
    tokens = blocks * size
    total_blocks = tiles.shape[2]
    key_block = (place - offset) * blocks + lax.broadcasted_iota(jnp.int32, (1, tokens), 1) // size
    query_block = place * blocks + lax.broadcasted_iota(jnp.int32, (blocks, 1), 0)
    key_doc = jnp.zeros((1, tokens), jnp.int32)
    query_doc = jnp.zeros((blocks, 1), jnp.int32)
    end = jnp.int32(0)
    for j in range(lengths.shape[1]):
        end = end + lengths[0, j]
        key_doc = key_doc + (key_block >= end).astype(jnp.int32)
        query_doc = query_doc + (query_block >= end).astype(jnp.int32)
    spread = lax.broadcasted_iota(jnp.int32, (total_blocks, tokens), 0) == key_block
    listed = jnp.dot(
        tiles[0].astype(jnp.float32).astype(jnp.bfloat16),
        spread.astype(jnp.float32).astype(jnp.bfloat16),
        preferred_element_type=jnp.float32,
    )
    allowed = (query_doc == key_doc) & (key_block <= query_block) & (key_block >= 0)
    allowed = allowed & ((listed > 0.5) | (key_block == query_block))
    bias[...] = jnp.where(allowed, 0.0, NEVER)


def place_kv(table, received, pack, place, offset, cap, keys, values, sem):
    packs = received.shape[0]
    ranks = lax.axis_size("ctx")
    size = received.shape[2] // cap
    source_place = jnp.maximum(place - offset, 0)
    for s in range(packs):
        for i in range(cap):
            slot = table[s * ranks + source_place, pack * cap + i]
            rows = pl.ds(pl.multiple_of(slot * size, size), size)
            block = pl.ds(i * size, size)
            pltpu.make_async_copy(received.at[s, 0, block], keys.at[rows], sem.at[0]).start()
            pltpu.make_async_copy(
                received.at[s, 1, block], values.at[rows, pl.ds(0, HEAD_WIDTH)], sem.at[1]
            ).start()
    values[:, HEAD_WIDTH:] = jnp.ones((values.shape[0], HEAD_WIDTH), jnp.bfloat16)


def wait_kv(keys, values, sem):
    half = values.at[:, pl.ds(0, HEAD_WIDTH)]
    pltpu.make_async_copy(keys, keys, sem.at[0]).wait()
    pltpu.make_async_copy(half, half, sem.at[1]).wait()


def place_q(table, received, pack, place, cap, queries, sem):
    packs = received.shape[0]
    ranks = lax.axis_size("ctx")
    size = received.shape[1] // cap
    for s in range(packs):
        for i in range(cap):
            slot = table[s * ranks + place, pack * cap + i]
            rows = pl.ds(pl.multiple_of(slot * size, size), size)
            pltpu.make_async_copy(
                received.at[s, pl.ds(i * size, size)], queries.at[rows], sem
            ).start()


def heads_as_rows(block):
    return jnp.concatenate(
        [block[:, h * HEAD_WIDTH:(h + 1) * HEAD_WIDTH] for h in range(QUERY_HEADS)], axis=0
    )


def heads_as_columns(rows, size):
    return jnp.concatenate(
        [rows[h * size:(h + 1) * size] for h in range(QUERY_HEADS)], axis=1
    )


def attend(query_rows, keys, values, bias):
    scores = lax.dot_general(
        query_rows, keys, (((1,), (1,)), ((), ())), preferred_element_type=jnp.float32
    )
    scores = scores * SCALE + bias
    top = jnp.maximum(jnp.max(scores, axis=1, keepdims=True), FLOOR)
    weights = jnp.exp2(scores - top).astype(jnp.bfloat16)
    return top, jnp.dot(weights, values, preferred_element_type=jnp.float32)


def own_kernel(
    cap, table, lengths, tiles, q_recv, kv_recv,
    out, state_o, state_l,
    queries, keys, values, bias, tri, stage, stage_o, stage_l, sem_in, sem_out, sem_state,
):
    place = lax.axis_index("ctx")
    pack = lax.axis_index("dp")
    tokens = queries.shape[0]
    blocks = bias.shape[0]
    size = tokens // blocks
    place_kv(table, kv_recv, pack, place, 0, cap, keys, values, sem_in)
    place_q(table, q_recv, pack, place, cap, queries, sem_in.at[2])
    fill_bias(bias, lengths, tiles, place, 0, blocks, size)
    row = lax.rem(lax.broadcasted_iota(jnp.int32, tri.shape[1:], 0), size)
    lane = lax.broadcasted_iota(jnp.int32, tri.shape[1:], 1)
    for parity in range(2):
        tri[parity] = jnp.where(lane - parity * size <= row, 0.0, NEVER)
    reads, _ = reach_of(lengths, place, 1, blocks)
    wait_kv(keys, values, sem_in)
    pltpu.make_async_copy(queries, queries, sem_in.at[2]).wait()

    copies = []
    for i in range(blocks):
        rows = slice(i * size, (i + 1) * size)
        width = (i // 2 + 1) * 2 * size
        query_rows = heads_as_rows(queries[rows, :])
        last = bias[i:i + 1, width - 2 * size:width] + tri[i % 2]
        scores = lax.dot_general(
            query_rows, keys[:width, :], (((1,), (1,)), ((), ())),
            preferred_element_type=jnp.float32,
        ) * SCALE
        tail = scores[:, width - 2 * size:] + last
        if width > 2 * size:
            head = scores[:, :width - 2 * size] + bias[i:i + 1, :width - 2 * size]
            scores = jnp.concatenate([head, tail], axis=1)
        else:
            scores = tail
        top = jnp.max(scores, axis=1, keepdims=True)
        weights = jnp.exp2(scores - top).astype(jnp.bfloat16)
        sums = jnp.dot(weights, values[:width, :], preferred_element_type=jnp.float32)
        denominator = sums[:, HEAD_WIDTH:]
        result = sums[:, :HEAD_WIDTH] / denominator
        stage[rows, :] = heads_as_columns(result, size).astype(jnp.bfloat16)
        group = pl.ds(i * QUERY_HEADS * size, QUERY_HEADS * size)
        stage_o[group, :] = result
        stage_l[group, :] = top + jnp.log2(denominator)
        copy = pltpu.make_async_copy(stage.at[rows], out.at[0, rows], sem_out.at[i])
        copy.start()
        copies.append(copy)

    @pl.when(reads > 0)
    def _():
        first = pltpu.make_async_copy(stage_o, state_o, sem_state.at[0])
        second = pltpu.make_async_copy(stage_l, state_l, sem_state.at[1])
        first.start()
        second.start()
        first.wait()
        second.wait()

    for copy in copies:
        copy.wait()


def hop_kernel(
    cap, offset, table, lengths, tiles, q_recv, kv_recv, out_in, state_o_in, state_l_in,
    out, state_o, state_l,
    queries, keys, values, bias, stage, stage_o, stage_l, sem_in, sem_state, sem_out, sem_back,
):
    place = lax.axis_index("ctx")
    pack = lax.axis_index("dp")
    tokens = queries.shape[0]
    blocks = bias.shape[0]
    size = tokens // blocks
    group = QUERY_HEADS * size
    reads, first = reach_of(lengths, place, offset, blocks)

    @pl.when(reads > 0)
    def _():
        place_kv(table, kv_recv, pack, place, offset, cap, keys, values, sem_in)
        place_q(table, q_recv, pack, place, cap, queries, sem_in.at[2])
        load_o = pltpu.make_async_copy(state_o_in, stage_o, sem_state.at[0])
        load_l = pltpu.make_async_copy(state_l_in, stage_l, sem_state.at[1])
        load_o.start()
        load_l.start()
        fill_bias(bias, lengths, tiles, place, offset, blocks, size)
        wait_kv(keys, values, sem_in)
        pltpu.make_async_copy(queries, queries, sem_in.at[2]).wait()
        load_o.wait()
        load_l.wait()

        def over(low):
            def step(i, carry):
                rows = pl.ds(pl.multiple_of(i * size, size), size)
                span = pl.ds(pl.multiple_of(i * group, group), group)
                query_rows = heads_as_rows(queries[rows, :])
                top, sums = attend(
                    query_rows, keys[low:, :], values[low:, :], bias[pl.ds(i, 1), low:]
                )
                before = stage_l[span, :]
                most = jnp.maximum(before, top)
                old = jnp.exp2(before - most)
                new = jnp.exp2(top - most)
                denominator = old + new * sums[:, HEAD_WIDTH:]
                result = (
                    old * stage_o[span, :] + new * sums[:, :HEAD_WIDTH]
                ) / denominator
                stage[rows, :] = heads_as_columns(result, size).astype(jnp.bfloat16)
                stage_o[span, :] = result
                stage_l[span, :] = most + jnp.log2(denominator)
                pltpu.make_async_copy(stage.at[rows], out.at[0, rows], sem_out).start()
                return carry

            lax.fori_loop(0, reads, step, 0)

        quarter = tokens // 4
        part = first // (blocks // 4)
        for n in range(4):
            pl.when(part == n)(functools.partial(over, n * quarter))

        def finish(i, carry):
            rows = pl.ds(pl.multiple_of(i * size, size), size)
            pltpu.make_async_copy(stage.at[rows], out.at[0, rows], sem_out).wait()
            return carry

        lax.fori_loop(0, reads, finish, 0)
        if offset == 1:
            store_o = pltpu.make_async_copy(stage_o, state_o, sem_back.at[0])
            store_l = pltpu.make_async_copy(stage_l, state_l, sem_back.at[1])
            store_o.start()
            store_l.start()
            store_o.wait()
            store_l.wait()


def per_device(queries, keys, values, dest_replica, dest_slot, doc_lengths, tile_mask):
    tokens = queries.shape[1]
    width = queries.shape[2]
    blocks = dest_replica.shape[1]
    size = tokens // blocks
    packs = lax.axis_size("dp")
    cap = blocks // packs
    bf16, f32 = jnp.bfloat16, jnp.float32
    rows = tokens * QUERY_HEADS
    params = pltpu.CompilerParams(vmem_limit_bytes=VMEM_LIMIT)

    def cost(flops, moved):
        return pl.CostEstimate(flops=flops, bytes_accessed=moved, transcendentals=0)

    kv_send, table = pl.pallas_call(
        functools.partial(pack_kv_kernel, cap),
        out_shape=(
            jax.ShapeDtypeStruct((packs, 2, cap * size, HEAD_WIDTH), bf16),
            jax.ShapeDtypeStruct((1, blocks), jnp.int32),
        ),
        in_specs=[SMEM, SMEM, ANY, ANY],
        out_specs=(ANY, SMEM),
        scratch_shapes=[pltpu.SMEM((packs,), jnp.int32), pltpu.SemaphoreType.DMA],
        cost_estimate=cost(0, 4 * tokens * HEAD_WIDTH * 2),
        name="pack_kv",
    )(dest_replica, dest_slot, keys, values)
    kv_recv = lax.all_to_all(kv_send, "dp", split_axis=0, concat_axis=0, tiled=True)
    table = lax.all_gather(table, ("dp", "ctx"), axis=0, tiled=True)
    q_send = pl.pallas_call(
        functools.partial(pack_q_kernel, cap),
        out_shape=jax.ShapeDtypeStruct((packs, cap * size, width), bf16),
        in_specs=[SMEM, ANY],
        out_specs=ANY,
        scratch_shapes=[pltpu.SMEM((packs,), jnp.int32), pltpu.SemaphoreType.DMA],
        cost_estimate=cost(0, 2 * tokens * width * 2),
        name="pack_q",
    )(dest_replica, queries)
    q_recv = lax.all_to_all(q_send, "dp", split_axis=0, concat_axis=0, tiled=True)

    state_shapes = (
        jax.ShapeDtypeStruct((1, tokens, width), bf16),
        jax.ShapeDtypeStruct((rows, HEAD_WIDTH), f32),
        jax.ShapeDtypeStruct((rows, HEAD_WIDTH), f32),
    )
    inputs = [
        pltpu.VMEM((tokens, width), bf16),
        pltpu.VMEM((tokens, HEAD_WIDTH), bf16),
        pltpu.VMEM((tokens, 2 * HEAD_WIDTH), bf16),
        pltpu.VMEM((blocks, tokens), f32),
    ]
    staged = [
        pltpu.VMEM((tokens, width), bf16),
        pltpu.VMEM((rows, HEAD_WIDTH), f32),
        pltpu.VMEM((rows, HEAD_WIDTH), f32),
    ]
    dma = pltpu.SemaphoreType.DMA
    state = pl.pallas_call(
        functools.partial(own_kernel, cap),
        out_shape=state_shapes,
        in_specs=[SMEM, SMEM, VMEM, ANY, ANY],
        out_specs=(ANY, ANY, ANY),
        scratch_shapes=inputs
        + [pltpu.VMEM((2, QUERY_HEADS * size, 2 * size), f32)]
        + staged
        + [dma((3,)), dma((blocks,)), dma((2,))],
        compiler_params=params,
        cost_estimate=cost(2 * 2 * rows * tokens * HEAD_WIDTH, 8 * tokens * width),
        name="attend_own",
    )(table, doc_lengths, tile_mask, q_recv, kv_recv)
    moving = kv_recv
    for offset in (1, 2):
        moving = shifted(moving, "ctx")
        state = pl.pallas_call(
            functools.partial(hop_kernel, cap, offset),
            out_shape=state_shapes,
            in_specs=[SMEM, SMEM, VMEM, ANY, ANY, ANY, ANY, ANY],
            out_specs=(ANY, ANY, ANY),
            scratch_shapes=inputs + staged + [dma((3,)), dma((2,)), dma, dma((2,))],
            input_output_aliases={5: 0, 6: 1, 7: 2},
            compiler_params=params,
            cost_estimate=cost(2 * 2 * rows * tokens * HEAD_WIDTH, 8 * tokens * width),
            name=f"attend_back_{offset}",
        )(table, doc_lengths, tile_mask, q_recv, moving, *state)
    return state[0]


def solution(mesh):
    return jax.shard_map(
        per_device,
        mesh=mesh,
        in_specs=(
            P("dp", "ctx", None),
            P("dp", "ctx", None),
            P("dp", "ctx", None),
            P("dp", "ctx"),
            P("dp", "ctx"),
            P("dp", None),
            P("dp", "ctx", None),
        ),
        out_specs=P("dp", "ctx", None),
        check_vma=False,
    )
```

time: 124 us -> 180 us (1.45)
  the two profiles are of different devices: /device:TPU:0 before, /device:TPU:31 now
where the time goes in v1:
time: 180 us; the launch traced here: 177 us
  Pallas kernels  82.8 us (46%)
  blocking collectives  69.4 us (39%)
  waiting for transfers between devices  13.8 us (8%)
  starting transfers between devices  11.3 us (6%)
    all_gather x1, blocking collectives, per_device(): table = lax.all_gather(table, ('dp', 'ctx'), axis=0, tiled=True)  69.4 us
    pallas_call x1, Pallas kernels, per_device(): pl.pallas_call(functools.partial(pack_q_kernel, cap), out_shape=jax.Shape...  33.7 us
    pallas_call x2, Pallas kernels, per_device(): pl.pallas_call(functools.partial(hop_kernel, cap, offset), out_shape=stat...  22.5 us
    pallas_call x1, Pallas kernels, per_device(): pl.pallas_call(functools.partial(pack_kv_kernel, cap), out_shape=(jax.Sha...  18.2 us
    ppermute x2, waiting for transfers between devices, shifted(): lax.ppermute(value, axis, [(source, source + 1) for source in range(count...  13.7 us
    pallas_call x1, Pallas kernels, per_device(): pl.pallas_call(functools.partial(own_kernel, cap), out_shape=state_shapes...  8.45 us
    all_to_all x1, starting transfers between devices, per_device(): lax.all_to_all(kv_send, 'dp', split_axis=0, concat_axis=0, tiled=True)  4.53 us
    all_to_all x1, starting transfers between devices, per_device(): lax.all_to_all(q_send, 'dp', split_axis=0, concat_axis=0, tiled=True)  4.21 us
  transfers between devices with their start and end apart: 4, of which 1 were waited for; matrix products, arithmetic and copies ran while one was open for 0% of the time, Pallas kernels for 31%

profile of v1, /device:TPU:31, one launch (start us, length us, event | category | flops | bytes accessed | tf_op | source)
XLA Modules:
  0.0 177.4 jit_solution(13125926205887687993)
XLA Ops:
  0.0 18.2 %pack_kv.1 = (bf16[8,2,128,128]{3,2,1,0:T(8,128)(2,1)}, s32[1,16]{1,0:T(1,128)}) custom-call(s32[1,16]{1,0:T(1,128)} %targets.3, s32[1,16]{1,0:T(1,128)} %slots.1, bf16[1,1024,128]{2,1,0:T(8,128)(2,1)} %keys.1, bf16[1,1024,128]{2,1,0:T(8,128)(2,1)} %values.1), custom_call_target="tpu_custom_call" | custom-call | bytes 1048576 | tf_op jit(solution)/shard_map/pack_kv/pallas_call | solution.py:317
  18.2 4.5 %all-to-all-start.1 = ((bf16[8,2,128,128]{3,2,1,0:T(8,128)(2,1)}), bf16[8,2,128,128]{3,2,1,0:T(8,128)(2,1)S(1)}, u32[]{:S(2)}, u32[]{:S(2)}) async-start(bf16[8,2,128,128]{3,2,1,0:T(8,128)(2,1)} %get-tuple-element.15), calls=%async_computation.1 | async-start | bytes 1048576 | tf_op jit(solution)/shard_map/all_to_all | solution.py:329
  22.7 0.0 copy-start.2
  22.7 0.0 copy-start
  22.7 0.0 copy-start.1
  22.7 33.7 %pack_q.1 = bf16[8,128,512]{2,1,0:T(8,128)(2,1)} custom-call(s32[1,16]{1,0:T(1,128)} %targets.3, bf16[1,1024,512]{2,1,0:T(8,128)(2,1)} %queries.1), custom_call_target="tpu_custom_call" | custom-call | bytes 2097152 | tf_op jit(solution)/shard_map/pack_q/pallas_call | solution.py:331
  56.4 0.0 all-to-all-done.1.kv_recv
  56.4 4.2 %all-to-all-start = ((bf16[8,128,512]{2,1,0:T(8,128)(2,1)}), bf16[8,128,512]{2,1,0:T(8,128)(2,1)S(1)}, u32[]{:S(2)}, u32[]{:S(2)}) async-start(bf16[8,128,512]{2,1,0:T(8,128)(2,1)} %pack_q.1), calls=%async_computation | async-start | bytes 2097152 | tf_op jit(solution)/shard_map/all_to_all | solution.py:340
  60.6 1.3 collective-permute-start
  61.9 13.7 %collective-permute-done.kv_recv = bf16[8,2,128,128]{3,2,1,0:T(8,128)(2,1)S(1)} collective-permute-done((bf16[8,2,128,128]{3,2,1,0:T(8,128)(2,1)S(1)}, bf16[8,2,128,128]{3,2,1,0:T(8,128)(2,1)S(1)}, u32[]{:S(2)}, u32[]{:S(2)}) %collective-permute-start) | collective-permute-done | bytes 524320 | tf_op jit(solution)/shard_map/ppermute | solution.py:24
  75.7 1.3 collective-permute-start.1
  77.0 0.0 copy-done.2
  77.0 69.4 %all-gather = s32[32,1,16]{2,1,0:T(1,128)S(1)} all-gather(s32[1,1,16]{2,1,0:T(1,128)S(1)} %bitcast.5), channel_id=1, replica_groups=mesh['dp'=8,'ctx'=4] {'dp','ctx'}, dimensions={0}, use_global_device_ids=true | all-gather | bytes 2112 | tf_op jit(solution)/shard_map/all_gather | solution.py:330
  146.4 0.0 all-to-all-done.q_recv
  146.4 0.0 copy-done
  146.4 0.0 copy-done.1
  146.4 8.4 %attend_own.1 = (bf16[1,1024,512]{2,1,0:T(8,128)(2,1)}, f32[4096,128]{1,0:T(8,128)S(1)}, f32[4096,128]{1,0:T(8,128)S(1)}) custom-call(s32[32,16]{1,0:T(8,128)S(1)} %bitcast.2, s32[1,16]{1,0:T(1,128)S(1)} %copy-done.1, s32[1,16,64]{2,1,0:T(8,128)S(1)} %copy-done, bf16[8,128,512]{2,1,0:T(8,128)(2,1)S(1)} %all-to-all-done.q_recv, ...), custom_call_target="tpu_custom_call" | custom-call | flops 2147483648 | bytes 4194304 | tf_op jit(solution)/shard_map/attend_own/pallas_call | solution.py:359
  154.9 12.8 %attend_back_1.1 = (bf16[1,1024,512]{2,1,0:T(8,128)(2,1)}, f32[4096,128]{1,0:T(8,128)S(1)}, f32[4096,128]{1,0:T(8,128)S(1)}) custom-call(s32[32,16]{1,0:T(8,128)S(1)} %bitcast.3, s32[1,16]{1,0:T(1,128)S(1)} %copy-done.1, s32[1,16,64]{2,1,0:T(8,128)S(1)} %copy-done, ...), custom_call_target="tpu_custom_call", output_to_operand_aliasing={{0}: (5, {}), {1}: (6, {}), {2}: (7, {})} | custom-call | flops 2147483648 | bytes 4194304 | tf_op jit(solution)/shard_map/attend_back_1/pallas_call | solution.py:375
  167.7 0.0 collective-permute-done.1.kv_recv
  167.7 9.7 %attend_back_2.1 = (bf16[1,1024,512]{2,1,0:T(8,128)(2,1)}, f32[4096,128]{1,0:T(8,128)S(1)}, f32[4096,128]{1,0:T(8,128)S(1)}) custom-call(s32[32,16]{1,0:T(8,128)S(1)} %bitcast.4, s32[1,16]{1,0:T(1,128)S(1)} %copy-done.1, s32[1,16,64]{2,1,0:T(8,128)S(1)} %copy-done, ...), custom_call_target="tpu_custom_call", output_to_operand_aliasing={{0}: (5, {}), {1}: (6, {}), {2}: (7, {})} | custom-call | flops 2147483648 | bytes 4194304 | tf_op jit(solution)/shard_map/attend_back_2/pallas_call | solution.py:375
Async XLA Ops:
  18.2 38.2 %all-to-all-start.1 = ((bf16[8,2,128,128]{3,2,1,0:T(8,128)(2,1)}), bf16[8,2,128,128]{3,2,1,0:T(8,128)(2,1)S(1)}, u32[]{:S(2)}, u32[]{:S(2)}) async-start(bf16[8,2,128,128]{3,2,1,0:T(8,128)(2,1)} %get-tuple-element.15), calls=%async_computation.1 | async-start | bytes 1048576 | tf_op jit(solution)/shard_map/all_to_all | solution.py:329
  22.7 54.2 %copy-start.2 = (s32[1,16]{1,0:T(1,128)S(1)}, s32[1,16]{1,0:T(1,128)}, u32[]{:S(2)}) copy-start(s32[1,16]{1,0:T(1,128)} %get-tuple-element.14) | copy-start | bytes 196
  22.7 123.7 %copy-start = (s32[1,16,64]{2,1,0:T(8,128)S(1)}, s32[1,16,64]{2,1,0:T(8,128)}, u32[]{:S(2)}) copy-start(s32[1,16,64]{2,1,0:T(8,128)} %tiles.5) | copy-start | bytes 12292
  22.7 123.7 %copy-start.1 = (s32[1,16]{1,0:T(1,128)S(1)}, s32[1,16]{1,0:T(1,128)}, u32[]{:S(2)}) copy-start(s32[1,16]{1,0:T(1,128)} %lengths.5) | copy-start | bytes 196
  56.4 90.0 %all-to-all-start = ((bf16[8,128,512]{2,1,0:T(8,128)(2,1)}), bf16[8,128,512]{2,1,0:T(8,128)(2,1)S(1)}, u32[]{:S(2)}, u32[]{:S(2)}) async-start(bf16[8,128,512]{2,1,0:T(8,128)(2,1)} %pack_q.1), calls=%async_computation | async-start | bytes 2097152 | tf_op jit(solution)/shard_map/all_to_all | solution.py:340
  60.6 15.0 %collective-permute-start = (bf16[8,2,128,128]{3,2,1,0:T(8,128)(2,1)S(1)}, bf16[8,2,128,128]{3,2,1,0:T(8,128)(2,1)S(1)}, u32[]{:S(2)}, u32[]{:S(2)}) collective-permute-start(bf16[8,2,128,128]{3,2,1,0:T(8,128)(2,1)S(1)} %all-to-all-done.1.kv_recv), channel_id=1, source_target_pairs={{0,1},{1,2},{2,3},{4,5},{5,6},{6,7},{8,9},{9,10},{10,11},{12,13},{... | collective-permute-start | bytes 1572872 | tf_op jit(solution)/shard_map/ppermute | solution.py:24
  75.7 92.0 %collective-permute-start.1 = (bf16[8,2,128,128]{3,2,1,0:T(8,128)(2,1)S(1)}, bf16[8,2,128,128]{3,2,1,0:T(8,128)(2,1)S(1)}, u32[]{:S(2)}, u32[]{:S(2)}) collective-permute-start(bf16[8,2,128,128]{3,2,1,0:T(8,128)(2,1)S(1)} %collective-permute-done.kv_recv), channel_id=1, source_target_pairs={{0,1},{1,2},{2,3},{4,5},{5,6},{6,7},{8,9},{9,10},{10,11},{12,13},{... | collective-permute-start | bytes 1572872 | tf_op jit(solution)/shard_map/ppermute | solution.py:24
